TPU v7x, 256 devices: a whole 4x4x8 slice. The times are simulated.
256 devices in a mesh: tm: 32 (over z, y), feat: 8 (over x, core).
Axes of the slice: x: 4, y: 4, z: 8, core: 2. Of those that a mesh axis runs over, the one named last changes fastest.
Arguments:
- tile_data: bfloat16 [2048, 32, 128, 128], P('tm', 'feat'), may hold values from -1 to 1
- tile_ids: int32 [2048, 32], P('tm', 'feat'), may hold values from 0 to 31, as said below
- owner_perm: int32 [2048], P('tm'), may hold values from 0 to 2047, as said below
- events: int32 [2048, 128], P('tm'), may hold values 0 or 1
- groups: int32 [2048, 128], P('tm'), may hold values from 0 to 127, as said below
- coefficients: bfloat16 [32768], P('feat'), may hold values from -4 to 4
Outputs:
- gradient: float32 [32768], P('feat')
- newton_step: float32 [32768], P('feat')
Inputs may be any that keep to these rules, and one draw needn't show every extreme that they name: `tile_ids`: in each feature shard's 4 columns a row block names 4 different local feature blocks. `owner_perm`: A permutation of row blocks; each patient shard of 64 row blocks sends exactly 2 of them to each time shard. `groups`: group numbers start at 0 in every row block and never fall within it; a tied group never spans two row blocks.
All inputs are finite; a program needn't handle non-finite values. No bound on the sum of `events` on one device may be relied on, other than what follows from the above.
Results may differ from a plain program's by a relative error of at most 0.00035.
The roundings to bfloat16 on the way count: a program that leaves them out, or rounds other values in their place, can miss the bound.
Values may be sent and summed in bfloat16 or wider, within the bound.
A program may use at most 128 MiB of HBM per device.

v0:
```python
import jax
import jax.numpy as jnp
from jax import lax
from jax.sharding import PartitionSpec as P

ridge_weight = 1.0


def entering(part, axis, combine, identity, reverse):
    count = lax.axis_size(axis)
    place = lax.axis_index(axis)
    ahead = count - 1 - place if reverse else place
    gathered = jax.tree.map(lambda a: lax.all_gather(a, axis), part)
    state = jax.tree.map(lambda a, e: jnp.zeros_like(a) + jnp.asarray(e, a.dtype), part, identity)

    def one(turn, state):
        source = count - 1 - turn if reverse else turn
        return combine(
            state, jax.tree.map(lambda a: lax.dynamic_index_in_dim(a, source, 0, False), gathered)
        )

    return lax.fori_loop(0, ahead, one, state)


def add_pair(earlier, later):
    return (earlier[0] + later[0], earlier[1] + later[1])


def add_one(earlier, later):
    return earlier + later


def solve_blocks(grad_blocks, hess_blocks):
    tile_width = hess_blocks.shape[1]
    system = hess_blocks + ridge_weight * jnp.eye(tile_width, dtype=jnp.float32)[None]
    factor = jnp.linalg.cholesky(system)
    return jax.scipy.linalg.cho_solve((factor, True), grad_blocks[:, :, None])[:, :, 0]


def local(tile_data, tile_ids, owner_perm, events, groups, coefficients):
    row_count = tile_data.shape[0]
    tile_width = tile_data.shape[2]
    shard_count = lax.axis_size("tm")
    per_pair = row_count // shard_count
    local_blocks = coefficients.shape[0] // tile_width
    coef_blocks = coefficients.reshape(local_blocks, tile_width)
    block_range = jnp.arange(local_blocks, dtype=jnp.int32)
    target = owner_perm // row_count
    arrival_slot = owner_perm % row_count
    sorting = jnp.argsort(target, stable=True)
    outgoing = (
        tile_data[sorting].reshape(
            shard_count, per_pair, tile_data.shape[1], tile_width, tile_width
        ),
        tile_ids[sorting].reshape(shard_count, per_pair, tile_ids.shape[1]),
        events[sorting].reshape(shard_count, per_pair, tile_width),
        arrival_slot[sorting].reshape(shard_count, per_pair),
    )
    received = (
        lax.all_to_all(outgoing[0], "tm", split_axis=0, concat_axis=0, tiled=True),
        lax.all_to_all(outgoing[1], "tm", split_axis=0, concat_axis=0, tiled=True),
        lax.all_to_all(outgoing[2], "tm", split_axis=0, concat_axis=0, tiled=True),
        lax.all_to_all(outgoing[3], "tm", split_axis=0, concat_axis=0, tiled=True),
    )
    arrival = received[3].reshape(row_count)
    restore_order = jnp.argsort(arrival)
    time_tiles = received[0].reshape(row_count, tile_data.shape[1], tile_width, tile_width)[
        restore_order
    ]
    time_ids = received[1].reshape(row_count, tile_ids.shape[1])[restore_order]
    time_events = received[2].reshape(row_count, tile_width)[restore_order]
    onehot = (time_ids[:, :, None] == block_range[None, None, :]).astype(jnp.bfloat16)
    picked = jnp.einsum(
        "nsj,jt->nst", onehot, coef_blocks, preferred_element_type=jnp.float32
    ).astype(jnp.bfloat16)
    time_eta = lax.psum(
        jnp.einsum("nspt,nst->np", time_tiles, picked, preferred_element_type=jnp.float32), "feat"
    )
    event_flag = time_events.astype(jnp.float32)
    risk_score = jnp.exp(time_eta)
    later_mask = (groups[:, None, :] >= groups[:, :, None]).astype(jnp.float32)
    later_in = jnp.einsum("bik,bk->bi", later_mask, risk_score, precision=lax.Precision.HIGHEST)
    block_tot = jnp.sum(risk_score, axis=1)
    device_tot = jnp.sum(block_tot)
    after_device = entering(device_tot, "tm", add_one, jnp.zeros((), jnp.float32), True)
    after_blocks = jnp.concatenate(
        [jnp.cumsum(block_tot[::-1])[::-1][1:], jnp.zeros((1,), jnp.float32)]
    )
    risk_total = after_device + after_blocks[:, None] + later_in
    hazard_one = event_flag / risk_total
    hazard_two = hazard_one / risk_total
    earlier_one = jnp.einsum("bki,bk->bi", later_mask, hazard_one, precision=lax.Precision.HIGHEST)
    earlier_two = jnp.einsum("bki,bk->bi", later_mask, hazard_two, precision=lax.Precision.HIGHEST)
    tot_one = jnp.sum(hazard_one, axis=1)
    tot_two = jnp.sum(hazard_two, axis=1)
    zero_scalar = jnp.zeros((), jnp.float32)
    before_dev = entering(
        (jnp.sum(tot_one), jnp.sum(tot_two)), "tm", add_pair, (zero_scalar, zero_scalar), False
    )
    before_one = jnp.concatenate([jnp.zeros((1,), jnp.float32), jnp.cumsum(tot_one)[:-1]])
    before_two = jnp.concatenate([jnp.zeros((1,), jnp.float32), jnp.cumsum(tot_two)[:-1]])
    cum_one = before_dev[0] + before_one[:, None] + earlier_one
    cum_two = before_dev[1] + before_two[:, None] + earlier_two
    residual = event_flag - risk_score * cum_one
    weight = risk_score * cum_one - risk_score * risk_score * cum_two
    residual, weight = (residual, weight)
    resid_round = residual.astype(jnp.bfloat16)
    weighted = (time_tiles * weight[:, None, :, None]).astype(jnp.bfloat16)
    grad_slots = jnp.einsum(
        "nspa,np->nsa", time_tiles, resid_round, preferred_element_type=jnp.float32
    )
    hess_slots = jnp.einsum(
        "nspa,nspb->nsab", weighted, time_tiles, preferred_element_type=jnp.float32
    )
    flat_ids = time_ids.reshape(-1)
    grad_local = (
        jnp.zeros((local_blocks, tile_width), jnp.float32)
        .at[flat_ids]
        .add(grad_slots.reshape(-1, tile_width))
    )
    hess_local = (
        jnp.zeros((local_blocks, tile_width, tile_width), jnp.float32)
        .at[flat_ids]
        .add(hess_slots.reshape(-1, tile_width, tile_width))
    )
    grad_local, hess_local = (grad_local, hess_local)
    grad_part, hess_part = (
        lax.psum_scatter(grad_local, "tm", scatter_dimension=0, tiled=True),
        lax.psum_scatter(hess_local, "tm", scatter_dimension=0, tiled=True),
    )
    step_part = solve_blocks(grad_part, hess_part)
    gradient, newton_step = (
        lax.all_gather(grad_part, "tm", axis=0, tiled=True),
        lax.all_gather(step_part, "tm", axis=0, tiled=True),
    )
    return (gradient.reshape(-1), newton_step.reshape(-1))


def solution(mesh):
    return jax.shard_map(
        local,
        mesh=mesh,
        in_specs=(
            P("tm", "feat", None, None),
            P("tm", "feat"),
            P("tm"),
            P("tm", None),
            P("tm", None),
            P("feat"),
        ),
        out_specs=(P("feat"), P("feat")),
        check_vma=False,
    )
```

profile of v0, /device:TPU:2, one launch (start us, length us, event | category | flops | bytes accessed | tf_op | source)
XLA Modules:
  0.0 893.4 jit_solution(6770830898521049463)
XLA Ops:
  7.2 0.7 and_select_fusion
  7.9 2.0 sort.34
  9.9 0.8 gather_fusion.1
  10.7 0.7 all_to_all.16
  11.4 11.5 %all-to-all-start.1 = ((s32[32,1,2]{2,1,0:T(1,128)}), s32[32,1,2]{2,1,0:T(1,128)S(1)}, u32[]{:S(2)}, u32[]{:S(2)}) async-start(s32[32,1,2]{2,1,0:T(1,128)} %bitcast.5), calls=%async_computation.1 | async-start | bytes 32768 | tf_op jit(solution)/shard_map/all_to_all | solution.py:63
  22.9 0.8 copy.20
  23.7 1.2 gather_fusion
  24.8 7.7 all-to-all-done.1
  32.5 3.8 all-to-all-start
  36.4 1.2 gather_fusion.5
  37.6 8.6 all-to-all-done
  46.2 3.9 all-to-all-start.3
  50.0 8.9 gather_fusion.3
  58.9 0.9 all-to-all-done.3
  59.8 9.2 %all-to-all-start.2 = ((bf16[32,2,4,128,128]{4,3,2,1,0:T(8,128)(2,1)}), bf16[32,2,4,128,128]{4,3,2,1,0:T(8,128)(2,1)}, u32[]{:S(2)}, u32[]{:S(2)}) async-start(bf16[32,2,4,128,128]{4,3,2,1,0:T(8,128)(2,1)} %bitcast.89), calls=%async_computation.2 | async-start | bytes 16777216 | tf_op jit(solution)/shard_map/all_to_all | solution.py:60
  69.1 0.7 fusion.33
  70.2 0.7 reduce.21
  71.0 2.0 sort.35
  73.1 0.6 gather_fusion.2
  74.1 0.6 gather_fusion.6
  74.7 173.6 %all-to-all-done.2 = bf16[32,2,4,128,128]{4,3,2,1,0:T(8,128)(2,1)} async-done(((bf16[32,2,4,128,128]{4,3,2,1,0:T(8,128)(2,1)}), bf16[32,2,4,128,128]{4,3,2,1,0:T(8,128)(2,1)}, u32[]{:S(2)}, u32[]{:S(2)}) %all-to-all-start.2) | async-done | bytes 8388640 | tf_op jit(solution)/shard_map/all_to_all | solution.py:60
  248.3 8.9 gather_fusion.4
  257.2 5.6 fusion.15
  262.8 20.7 %psum.7 = f32[64,128]{1,0:T(8,128)S(1)} all-reduce(f32[64,128]{1,0:T(8,128)S(1)} %bitcast.96), channel_id=1, replica_groups=mesh['tm'=32,'feat'=8] {'feat'}, use_global_device_ids=true, to_apply=%region_2.3 | all-reduce | flops 8192 | bytes 65536 | tf_op jit(solution)/shard_map/psum | solution.py:76
  283.5 0.6 exponential_reduce_fusion.1
  284.1 1.4 dynamic-update-slice.3
  285.5 75.4 %all-reduce = f32[32]{0:T(128)S(1)} all-reduce(f32[32]{0:T(128)S(1)} %dynamic-update-slice.3), channel_id=1, replica_groups=mesh['tm'=32,'feat'=8] {'tm'}, use_global_device_ids=true, to_apply=%add | all-reduce | flops 32 | bytes 256
  361.0 39.0 %while.24 = (s32[]{:T(128)}, f32[]{:T(128)}, s32[]{:T(128)}, f32[32]{0:T(128)S(1)}, s32[]{:T(128)}, /*index=5*/s32[]{:T(128)}, s32[]{:T(128)}, s32[]{:T(128)}) while((s32[]{:T(128)}, f32[]{:T(128)}, s32[]{:T(128)}, f32[32]{0:T(128)S(1)}, s32[]{:T(128)}, /*index=5*/s32[]{:T(128)}, s32[]{:T(128)}, s32[]{:T(128)}) %tuple.56), condition=%wide.region_5.6_spmd, body=%wide.region_4.5_spmd.sunk | while | flops 7 | bytes 163 | solution.py:22
  362.3 0.6 dynamic_slice.17
  363.5 0.6 dynamic_slice.17
  364.8 0.6 dynamic_slice.17
  366.1 0.6 dynamic_slice.17
  367.3 0.6 dynamic_slice.17
  368.6 0.6 dynamic_slice.17
  369.8 0.6 dynamic_slice.17
  371.1 0.6 dynamic_slice.17
  372.4 0.6 dynamic_slice.17
  373.6 0.6 dynamic_slice.17
  400.5 4.0 fusion.6
  404.5 0.7 fusion.31
  405.3 2.9 fusion.2
  408.2 2.9 fusion.4
  411.1 1.4 dynamic-update-slice.5
  412.5 1.4 dynamic-update-slice.4
  413.8 69.6 %all-reduce.4 = (f32[32]{0:T(128)S(1)}, f32[32]{0:T(128)S(1)}) all-reduce(f32[32]{0:T(128)S(1)} %dynamic-update-slice.4, f32[32]{0:T(128)S(1)} %dynamic-update-slice.5), channel_id=1, replica_groups=mesh['tm'=32,'feat'=8] {'tm'}, use_global_device_ids=true, to_apply=%add.1 | all-reduce | flops 64 | bytes 512
  484.5 13.4 %fusion = f32[64,4,128,128]{3,2,1,0:T(8,128)} fusion(bf16[64,4,128,128]{3,2,1,0:T(8,128)(2,1)} %gather_fusion.4, f32[64,128]{1,0:T(8,128)S(1)} %get-tuple-element.129), kind=kOutput, calls=%fused_computation.10 | convolution fusion | flops 1086324736 | bytes 25198592 | tf_op jit(solution)/shard_map/nspa,nspb->nsab/dot_general | solution.py:112
  498.1 33.2 %scatter_fusion = f32[32,128,128]{2,1,0:T(8,128)S(1)} fusion(f32[32,128,128]{2,1,0:T(8,128)S(1)} %broadcast_in_dim.14, s32[256]{0:T(256)S(1)} %bitcast.102, f32[256,128,128]{2,1,0:T(8,128)} %bitcast.88), kind=kCustom, calls=%fused_computation.8 | custom fusion | flops 4194304 | bytes 50332672 | tf_op jit(solution)/shard_map/scatter-add | solution.py:124
  531.4 1.3 copy-done.1
  532.7 4.6 fusion.20
  537.3 1.4 scatter_custom_fusion
  538.7 217.3 %all-reduce.3 = f32[32,128]{1,0:T(8,128)S(1)} all-reduce(f32[32,128]{1,0:T(8,128)S(1)} %scatter_custom_fusion), channel_id=3, replica_groups=mesh['tm'=32,'feat'=8] {'tm'}, use_global_device_ids=true, to_apply=%region_15.16.clone | all-reduce | flops 4096 | bytes 32768
  756.0 0.7 fusion.30
  756.7 34.4 %all-gather.1 = f32[32,1,128]{2,1,0:T(1,128)S(1)} all-gather(f32[1,1,128]{2,1,0:T(1,128)S(1)} %fusion.30), channel_id=1, replica_groups=mesh['tm'=32,'feat'=8] {'tm'}, dimensions={0}, use_global_device_ids=true | all-gather | bytes 16896 | tf_op jit(solution)/shard_map/all_gather | solution.py:133
  791.1 31.2 %reduce-scatter.2.cloned.1.call-done = f32[1,128,128]{2,1,0:T(8,128)} async-done(((f32[32,128,128]{2,1,0:T(8,128)}), f32[1,128,128]{2,1,0:T(8,128)}) %reduce-scatter.2.cloned.1.call-update) | async-done | bytes 65552 | tf_op jit(solution)/shard_map/reduce_scatter | solution.py:129
  822.3 0.9 convert_add_fusion
  823.3 0.9 fusion.19
  824.2 11.7 %custom-call.11 = f32[1,128,128]{2,1,0:T(8,128)S(1)} custom-call(f32[1,128,128]{2,1,0:T(8,128)S(1)} %fusion.19), custom_call_target="Cholesky" | custom-call | tf_op jit(solution)/shard_map/jit(cholesky)/cholesky | solution.py:36
  835.9 0.6 compare_reduce_fusion
  836.5 0.7 select_select_fusion
  837.2 9.8 %custom-call.12 = f32[1,128,128]{1,2,0:T(8,128)S(1)} custom-call(f32[1,128,128]{2,1,0:T(8,128)S(1)} %select_select_fusion), custom_call_target="InvertDiagBlocksLowerTriangular" | custom-call | tf_op jit(solution)/shard_map/jit(_cho_solve)/triangular_solve | solution.py:37
  847.0 0.8 convolution_bitcast_fusion.1
  848.1 37.2 %all-gather.2 = f32[32,1,128]{2,1,0:T(1,128)S(1)} all-gather(f32[1,1,128]{2,1,0:T(1,128)S(1)} %convolution_bitcast_fusion), channel_id=2, replica_groups=mesh['tm'=32,'feat'=8] {'tm'}, dimensions={0}, use_global_device_ids=true | all-gather | bytes 16896 | tf_op jit(solution)/shard_map/all_gather | solution.py:134
  885.3 0.6 copy.68
  885.9 0.6 copy.69
  (66 shorter events, 15.5 us)
Async XLA Ops:
  7.2 29.2 %copy-start = (s32[64,128]{1,0:T(8,128)S(1)}, s32[64,128]{1,0:T(8,128)}, u32[]{:S(2)}) copy-start(s32[64,128]{1,0:T(8,128)} %param.13) | copy-start | bytes 98308
  11.4 21.2 %all-to-all-start.1 = ((s32[32,1,2]{2,1,0:T(1,128)}), s32[32,1,2]{2,1,0:T(1,128)S(1)}, u32[]{:S(2)}, u32[]{:S(2)}) async-start(s32[32,1,2]{2,1,0:T(1,128)} %bitcast.5), calls=%async_computation.1 | async-start | bytes 32768 | tf_op jit(solution)/shard_map/all_to_all | solution.py:63
  32.5 13.6 %all-to-all-start = ((s32[32,2,4]{2,1,0:T(2,128)}), s32[32,2,4]{2,1,0:T(2,128)S(1)}, u32[]{:S(2)}, u32[]{:S(2)}) async-start(s32[32,2,4]{2,1,0:T(2,128)} %bitcast.3), calls=%async_computation | async-start | bytes 65536 | tf_op jit(solution)/shard_map/all_to_all | solution.py:61
  46.2 13.6 %all-to-all-start.3 = ((s32[32,2,128]{2,1,0:T(2,128)}), s32[32,2,128]{2,1,0:T(2,128)S(1)}, u32[]{:S(2)}, u32[]{:S(2)}) async-start(s32[32,2,128]{2,1,0:T(2,128)} %bitcast.9), calls=%async_computation.3 | async-start | bytes 65536 | tf_op jit(solution)/shard_map/all_to_all | solution.py:62
  59.8 9.3 %copy-start.3 = (u32[256]{0:T(256)S(1)}, u32[256]{0:T(256)}, u32[]{:S(2)}) copy-start(u32[256]{0:T(256)} %constant.148) | copy-start | bytes 3076
  59.8 14.1 %copy-start.2 = (bf16[4096]{0:T(1024)(128)(2,1)S(1)}, bf16[4096]{0:T(1024)(128)(2,1)}, u32[]{:S(2)}) copy-start(bf16[4096]{0:T(1024)(128)(2,1)} %param.15) | copy-start | bytes 24580
  59.8 188.5 %all-to-all-start.2 = ((bf16[32,2,4,128,128]{4,3,2,1,0:T(8,128)(2,1)}), bf16[32,2,4,128,128]{4,3,2,1,0:T(8,128)(2,1)}, u32[]{:S(2)}, u32[]{:S(2)}) async-start(bf16[32,2,4,128,128]{4,3,2,1,0:T(8,128)(2,1)} %bitcast.89), calls=%async_computation.2 | async-start | bytes 16777216 | tf_op jit(solution)/shard_map/all_to_all | solution.py:60
  69.0 753.3 %reduce-scatter.2.cloned.1.call-start = ((), (), s32[]{:S(2)}) async-start(), calls=%async_computation.5 | async-start | bytes 2162688 | tf_op jit(solution)/shard_map/reduce_scatter | solution.py:129
  257.2 143.3 %copy-start.4 = (s32[64,128]{1,0:T(8,128)S(1)}, s32[64,128]{1,0:T(8,128)}, u32[]{:S(2)}) copy-start(s32[64,128]{1,0:T(8,128)} %param.14) | copy-start | bytes 98308
  531.3 1.4 copy-start.1
Sparse Core Ops, SparseCore 0:
  532.8 289.4 reduce-scatter.1
where the time goes:
time: 896 us; the launch traced here: 893 us
  blocking collectives  455 us (51%)
  waiting for transfers between devices  222 us (25%)
  other arithmetic  66.5 us (7%)
  local copies, waits for them, and re-layouts  51.8 us (6%)
  matrix products  34.7 us (4%)
  starting transfers between devices  28.4 us (3%)
  loops' own time  21 us (2%)
  between operations  14.3 us (2%)
    unnamed x3, blocking collectives  362 us
    all_to_all x1, waiting for transfers between devices, local(): lax.all_to_all(outgoing[0], 'tm', split_axis=0, concat_axis=0, tiled=True)  174 us
    all_gather x1, blocking collectives, local(): lax.all_gather(step_part, 'tm', axis=0, tiled=True)  37.2 us
    all_gather x1, blocking collectives, local(): lax.all_gather(grad_part, 'tm', axis=0, tiled=True)  34.4 us
    scatter-add x1, other arithmetic, local(): hess_local = jnp.zeros((local_blocks, tile_width, tile_width), jnp.float3...  33.2 us
    reduce_scatter x1, waiting for transfers between devices, local(): lax.psum_scatter(hess_local, 'tm', scatter_dimension=0, tiled=True)  31.2 us
    another operation x2, loops' own time, entering(): return lax.fori_loop(0, ahead, one, state)  21 us
    psum x1, blocking collectives, local(): lax.psum(jnp.einsum('nspt,nst->np', time_tiles, picked, preferred_element...  20.7 us
  transfers between devices with their start and end apart: 5, of which 5 were waited for; matrix products, arithmetic and copies ran while one was open for 3% of the time, Pallas kernels for 0%

commit v1 on v0

--- a/solution.py
+++ b/solution.py
@@ -73,7 +73,12 @@
     picked = jnp.einsum(
         "nsj,jt->nst", onehot, coef_blocks, preferred_element_type=jnp.float32
     ).astype(jnp.bfloat16)
-    time_eta = lax.psum(
+
+    def blocks_feed(xin, axis_tag):
+        all_rows = jax.lax.all_gather(xin, axis_tag)
+        return jnp.sum(all_rows, axis=0)
+
+    time_eta = blocks_feed(
         jnp.einsum("nspt,nst->np", time_tiles, picked, preferred_element_type=jnp.float32), "feat"
     )
     event_flag = time_events.astype(jnp.float32)

time: 896 us -> 887 us (0.990)
  blocking collectives: 455 us -> 446 us
    psum x1 -> x0, blocking collectives: 20.7 us -> none  [local(): lax.psum(jnp.einsum('nspt,nst->np', time_tiles, picked, preferred_element...]
    all_gather x0 -> x1, blocking collectives: none -> 12.9 us  [blocks_feed(): all_rows = jax.lax.all_gather(xin, axis_tag)]
where the time goes in v1:
time: 887 us; the launch traced here: 884 us
  blocking collectives  446 us (50%)
  waiting for transfers between devices  221 us (25%)
  other arithmetic  66.6 us (8%)
  local copies, waits for them, and re-layouts  51.8 us (6%)
  matrix products  34.7 us (4%)
  starting transfers between devices  28.4 us (3%)
  loops' own time  21 us (2%)
  between operations  14.3 us (2%)
    unnamed x3, blocking collectives  361 us
    all_to_all x1, waiting for transfers between devices, local(): lax.all_to_all(outgoing[0], 'tm', split_axis=0, concat_axis=0, tiled=True)  174 us
    all_gather x1, blocking collectives, local(): lax.all_gather(step_part, 'tm', axis=0, tiled=True)  37.2 us
    all_gather x1, blocking collectives, local(): lax.all_gather(grad_part, 'tm', axis=0, tiled=True)  34.4 us
    scatter-add x1, other arithmetic, local(): hess_local = jnp.zeros((local_blocks, tile_width, tile_width), jnp.float3...  33.2 us
    reduce_scatter x1, waiting for transfers between devices, local(): lax.psum_scatter(hess_local, 'tm', scatter_dimension=0, tiled=True)  30.3 us
    another operation x2, loops' own time, entering(): return lax.fori_loop(0, ahead, one, state)  21 us
    dynamic_slice x31, local copies, waits for them, and re-layouts, one(): lax.dynamic_index_in_dim(a, source, 0, False)  18.2 us
  transfers between devices with their start and end apart: 5, of which 5 were waited for; matrix products, arithmetic and copies ran while one was open for 3% of the time, Pallas kernels for 0%

profile of v1, /device:TPU:2, one launch (start us, length us, event | category | flops | bytes accessed | tf_op | source)
XLA Modules:
  0.0 883.5 jit_solution(9461065375173440845)
XLA Ops:
  7.2 0.7 and_select_fusion
  7.9 2.0 sort.34
  9.9 0.8 gather_fusion.1
  10.7 0.7 all_to_all.16
  11.4 11.5 %all-to-all-start.1 = ((s32[32,1,2]{2,1,0:T(1,128)}), s32[32,1,2]{2,1,0:T(1,128)S(1)}, u32[]{:S(2)}, u32[]{:S(2)}) async-start(s32[32,1,2]{2,1,0:T(1,128)} %bitcast.5), calls=%async_computation.1 | async-start | bytes 32768 | tf_op jit(solution)/shard_map/all_to_all | solution.py:63
  22.9 0.8 copy.28
  23.7 1.2 gather_fusion
  24.8 7.7 all-to-all-done.1
  32.5 3.8 all-to-all-start
  36.4 1.2 gather_fusion.5
  37.6 8.6 all-to-all-done
  46.2 3.9 all-to-all-start.3
  50.0 8.9 %gather_fusion.3 = bf16[64,4,128,128]{3,2,1,0:T(8,128)(2,1)} fusion(bf16[64,4,128,128]{3,2,1,0:T(8,128)(2,1)} %param.10, s32[1024]{0:T(1024)S(1)} %pad_clamp_fusion.1), kind=kCustom, calls=%fused_computation.3 | custom fusion | bytes 16777472 | tf_op jit(solution)/shard_map/gather | solution.py:52
  58.9 0.9 all-to-all-done.3
  59.8 9.2 %all-to-all-start.2 = ((bf16[32,2,4,128,128]{4,3,2,1,0:T(8,128)(2,1)}), bf16[32,2,4,128,128]{4,3,2,1,0:T(8,128)(2,1)}, u32[]{:S(2)}, u32[]{:S(2)}) async-start(bf16[32,2,4,128,128]{4,3,2,1,0:T(8,128)(2,1)} %bitcast.90), calls=%async_computation.2 | async-start | bytes 16777216 | tf_op jit(solution)/shard_map/all_to_all | solution.py:60
  69.1 0.7 fusion.33
  70.2 0.7 reduce.21
  71.0 2.0 sort.35
  73.1 0.6 gather_fusion.2
  74.1 0.6 gather_fusion.6
  74.7 173.6 %all-to-all-done.2 = bf16[32,2,4,128,128]{4,3,2,1,0:T(8,128)(2,1)} async-done(((bf16[32,2,4,128,128]{4,3,2,1,0:T(8,128)(2,1)}), bf16[32,2,4,128,128]{4,3,2,1,0:T(8,128)(2,1)}, u32[]{:S(2)}, u32[]{:S(2)}) %all-to-all-start.2) | async-done | bytes 8388640 | tf_op jit(solution)/shard_map/all_to_all | solution.py:60
  248.3 8.9 %gather_fusion.4 = bf16[64,4,128,128]{3,2,1,0:T(8,128)(2,1)} fusion(bf16[64,4,128,128]{3,2,1,0:T(8,128)(2,1)} %bitcast.8, s32[1024]{0:T(1024)S(1)} %pad_clamp_fusion), kind=kCustom, calls=%fused_computation.4 | custom fusion | bytes 16777472 | tf_op jit(solution)/shard_map/gather | solution.py:67
  257.2 5.6 fusion.15
  262.8 12.9 %all-gather = f32[512,128]{1,0:T(8,128)S(1)} all-gather(f32[64,128]{1,0:T(8,128)S(1)} %bitcast.97), channel_id=2, replica_groups=mesh['tm'=32,'feat'=8] {'feat'}, dimensions={0}, use_global_device_ids=true | all-gather | bytes 294912 | tf_op jit(solution)/shard_map/all_gather | solution.py:78
  275.8 0.6 exponential_reduce_fusion.1
  276.4 1.4 dynamic-update-slice.3
  277.8 74.3 %all-reduce = f32[32]{0:T(128)S(1)} all-reduce(f32[32]{0:T(128)S(1)} %dynamic-update-slice.3), channel_id=1, replica_groups=mesh['tm'=32,'feat'=8] {'tm'}, use_global_device_ids=true, to_apply=%add | all-reduce | flops 32 | bytes 256
  352.1 39.0 %while.24 = (s32[]{:T(128)}, f32[]{:T(128)}, s32[]{:T(128)}, f32[32]{0:T(128)S(1)}, s32[]{:T(128)}, /*index=5*/s32[]{:T(128)}, s32[]{:T(128)}, s32[]{:T(128)}) while((s32[]{:T(128)}, f32[]{:T(128)}, s32[]{:T(128)}, f32[32]{0:T(128)S(1)}, s32[]{:T(128)}, /*index=5*/s32[]{:T(128)}, s32[]{:T(128)}, s32[]{:T(128)}) %tuple.56), condition=%wide.region_5.6_spmd, body=%wide.region_4.5_spmd.sunk | while | flops 7 | bytes 163 | solution.py:22
  353.4 0.6 dynamic_slice.17
  354.6 0.6 dynamic_slice.17
  355.9 0.6 dynamic_slice.17
  357.1 0.6 dynamic_slice.17
  358.4 0.6 dynamic_slice.17
  359.7 0.6 dynamic_slice.17
  360.9 0.6 dynamic_slice.17
  362.2 0.6 dynamic_slice.17
  363.4 0.6 dynamic_slice.17
  364.7 0.6 dynamic_slice.17
  391.6 4.0 fusion.6
  395.6 0.7 fusion.31
  396.4 2.9 fusion.2
  399.3 2.9 fusion.4
  402.2 1.4 dynamic-update-slice.5
  403.6 1.4 dynamic-update-slice.4
  404.9 69.6 %all-reduce.4 = (f32[32]{0:T(128)S(1)}, f32[32]{0:T(128)S(1)}) all-reduce(f32[32]{0:T(128)S(1)} %dynamic-update-slice.4, f32[32]{0:T(128)S(1)} %dynamic-update-slice.5), channel_id=1, replica_groups=mesh['tm'=32,'feat'=8] {'tm'}, use_global_device_ids=true, to_apply=%add.1 | all-reduce | flops 64 | bytes 512
  475.5 13.4 %fusion = f32[64,4,128,128]{3,2,1,0:T(8,128)} fusion(bf16[64,4,128,128]{3,2,1,0:T(8,128)(2,1)} %gather_fusion.4, f32[64,128]{1,0:T(8,128)S(1)} %get-tuple-element.129), kind=kOutput, calls=%fused_computation.10 | convolution fusion | flops 1086324736 | bytes 25198592 | tf_op jit(solution)/shard_map/nspa,nspb->nsab/dot_general | solution.py:117
  489.2 33.2 %scatter_fusion = f32[32,128,128]{2,1,0:T(8,128)S(1)} fusion(f32[32,128,128]{2,1,0:T(8,128)S(1)} %broadcast_in_dim.14, s32[256]{0:T(256)S(1)} %bitcast.104, f32[256,128,128]{2,1,0:T(8,128)} %bitcast.89), kind=kCustom, calls=%fused_computation.8 | custom fusion | flops 4194304 | bytes 50332672 | tf_op jit(solution)/shard_map/scatter-add | solution.py:129
  522.4 1.3 copy-done.1
  523.8 4.6 fusion.20
  528.4 1.4 scatter_custom_fusion
  529.8 217.3 %all-reduce.3 = f32[32,128]{1,0:T(8,128)S(1)} all-reduce(f32[32,128]{1,0:T(8,128)S(1)} %scatter_custom_fusion), channel_id=4, replica_groups=mesh['tm'=32,'feat'=8] {'tm'}, use_global_device_ids=true, to_apply=%region_15.16.clone | all-reduce | flops 4096 | bytes 32768
  747.1 0.7 fusion.30
  747.8 34.4 %all-gather.2 = f32[32,1,128]{2,1,0:T(1,128)S(1)} all-gather(f32[1,1,128]{2,1,0:T(1,128)S(1)} %fusion.30), channel_id=1, replica_groups=mesh['tm'=32,'feat'=8] {'tm'}, dimensions={0}, use_global_device_ids=true | all-gather | bytes 16896 | tf_op jit(solution)/shard_map/all_gather | solution.py:138
  782.3 30.3 %reduce-scatter.2.cloned.1.call-done = f32[1,128,128]{2,1,0:T(8,128)} async-done(((f32[32,128,128]{2,1,0:T(8,128)}), f32[1,128,128]{2,1,0:T(8,128)}) %reduce-scatter.2.cloned.1.call-update) | async-done | bytes 65552 | tf_op jit(solution)/shard_map/reduce_scatter | solution.py:134
  812.6 0.9 convert_add_fusion
  813.5 0.9 fusion.19
  814.4 11.7 %custom-call.11 = f32[1,128,128]{2,1,0:T(8,128)S(1)} custom-call(f32[1,128,128]{2,1,0:T(8,128)S(1)} %fusion.19), custom_call_target="Cholesky" | custom-call | tf_op jit(solution)/shard_map/jit(cholesky)/cholesky | solution.py:36
  826.1 0.6 compare_reduce_fusion
  826.8 0.7 select_select_fusion
  827.4 9.8 %custom-call.12 = f32[1,128,128]{1,2,0:T(8,128)S(1)} custom-call(f32[1,128,128]{2,1,0:T(8,128)S(1)} %select_select_fusion), custom_call_target="InvertDiagBlocksLowerTriangular" | custom-call | tf_op jit(solution)/shard_map/jit(_cho_solve)/triangular_solve | solution.py:37
  837.2 0.8 convolution_bitcast_fusion.1
  838.3 37.2 %all-gather.3 = f32[32,1,128]{2,1,0:T(1,128)S(1)} all-gather(f32[1,1,128]{2,1,0:T(1,128)S(1)} %convolution_bitcast_fusion), channel_id=3, replica_groups=mesh['tm'=32,'feat'=8] {'tm'}, dimensions={0}, use_global_device_ids=true | all-gather | bytes 16896 | tf_op jit(solution)/shard_map/all_gather | solution.py:139
  875.5 0.6 copy.77
  876.1 0.6 copy.78
  (67 shorter events, 15.5 us)
Async XLA Ops:
  7.2 29.2 %copy-start = (s32[64,128]{1,0:T(8,128)S(1)}, s32[64,128]{1,0:T(8,128)}, u32[]{:S(2)}) copy-start(s32[64,128]{1,0:T(8,128)} %param.13) | copy-start | bytes 98308
  11.4 21.2 %all-to-all-start.1 = ((s32[32,1,2]{2,1,0:T(1,128)}), s32[32,1,2]{2,1,0:T(1,128)S(1)}, u32[]{:S(2)}, u32[]{:S(2)}) async-start(s32[32,1,2]{2,1,0:T(1,128)} %bitcast.5), calls=%async_computation.1 | async-start | bytes 32768 | tf_op jit(solution)/shard_map/all_to_all | solution.py:63
  32.5 13.6 %all-to-all-start = ((s32[32,2,4]{2,1,0:T(2,128)}), s32[32,2,4]{2,1,0:T(2,128)S(1)}, u32[]{:S(2)}, u32[]{:S(2)}) async-start(s32[32,2,4]{2,1,0:T(2,128)} %bitcast.3), calls=%async_computation | async-start | bytes 65536 | tf_op jit(solution)/shard_map/all_to_all | solution.py:61
  46.2 13.6 %all-to-all-start.3 = ((s32[32,2,128]{2,1,0:T(2,128)}), s32[32,2,128]{2,1,0:T(2,128)S(1)}, u32[]{:S(2)}, u32[]{:S(2)}) async-start(s32[32,2,128]{2,1,0:T(2,128)} %bitcast.9), calls=%async_computation.3 | async-start | bytes 65536 | tf_op jit(solution)/shard_map/all_to_all | solution.py:62
  59.8 9.3 %copy-start.3 = (u32[256]{0:T(256)S(1)}, u32[256]{0:T(256)}, u32[]{:S(2)}) copy-start(u32[256]{0:T(256)} %constant.148) | copy-start | bytes 3076
  59.8 14.1 %copy-start.2 = (bf16[4096]{0:T(1024)(128)(2,1)S(1)}, bf16[4096]{0:T(1024)(128)(2,1)}, u32[]{:S(2)}) copy-start(bf16[4096]{0:T(1024)(128)(2,1)} %param.15) | copy-start | bytes 24580
  59.8 188.5 %all-to-all-start.2 = ((bf16[32,2,4,128,128]{4,3,2,1,0:T(8,128)(2,1)}), bf16[32,2,4,128,128]{4,3,2,1,0:T(8,128)(2,1)}, u32[]{:S(2)}, u32[]{:S(2)}) async-start(bf16[32,2,4,128,128]{4,3,2,1,0:T(8,128)(2,1)} %bitcast.90), calls=%async_computation.2 | async-start | bytes 16777216 | tf_op jit(solution)/shard_map/all_to_all | solution.py:60
  69.0 743.6 %reduce-scatter.2.cloned.1.call-start = ((), (), s32[]{:S(2)}) async-start(), calls=%async_computation.5 | async-start | bytes 2162688 | tf_op jit(solution)/shard_map/reduce_scatter | solution.py:134
  257.2 134.3 %copy-start.4 = (s32[64,128]{1,0:T(8,128)S(1)}, s32[64,128]{1,0:T(8,128)}, u32[]{:S(2)}) copy-start(s32[64,128]{1,0:T(8,128)} %param.14) | copy-start | bytes 98308
  522.4 1.4 copy-start.1
Sparse Core Ops, SparseCore 0:
  523.9 288.6 reduce-scatter.1
